TPU v7x, 32 devices: a whole 2x2x4 slice. The times are simulated.
32 devices in a mesh: dp: 8 (over z, y), tensor: 4 (over x, core).
Axes of the slice: x: 2, y: 2, z: 4, core: 2. Of those that a mesh axis runs over, the one named last changes fastest.
Arguments:
- block_input: bfloat16 [4096, 2048], P(('dp', 'tensor')), may hold values from -6 to 6
- cotangent: bfloat16 [4096, 2048], P(('dp', 'tensor')), may hold values from -6 to 6
- sequence_blocks: int32 [2], replicated, may hold values from 4 to 12, as said below
- gain_attention: float32 [2048], replicated, may hold values from 0.5 to 1.5
- query_weight: bfloat16 [2048, 2048], P(None, 'tensor'), may hold values from -0.125 to 0.125
- keyval_weight: bfloat16 [2048, 256], replicated, may hold values from -0.125 to 0.125
- output_weight: bfloat16 [2048, 2048], P(None, 'tensor'), may hold values from -2 to 2
- gain_feedforward: float32 [2048], replicated, may hold values from 0.5 to 1.5
- gate_weight: bfloat16 [2048, 6144], P(None, 'tensor'), may hold values from -0.125 to 0.125
- up_weight: bfloat16 [2048, 6144], P(None, 'tensor'), may hold values from -0.125 to 0.125
- down_weight: bfloat16 [2048, 6144], P(None, 'tensor'), may hold values from -0.078125 to 0.078125
Outputs:
- block_output: bfloat16 [4096, 2048], P(('dp', 'tensor'))
- grad_input: float32 [4096, 2048], P(('dp', 'tensor'))
- grad_gain_attention: float32 [2048], P('dp')
- grad_query: float32 [2048, 2048], P('dp', 'tensor')
- grad_keyval: float32 [2048, 256], P('dp')
- grad_output_weight: float32 [2048, 2048], P('dp', 'tensor')
- grad_gain_feedforward: float32 [2048], P('dp')
- grad_gate: float32 [2048, 6144], P('dp', 'tensor')
- grad_up: float32 [2048, 6144], P('dp', 'tensor')
- grad_down: float32 [2048, 6144], P('dp', 'tensor')
Inputs may be any that keep to these rules, and one draw needn't show every extreme that they name: Sequence n is sequence_blocks[n] whole blocks of 256 tokens; the 2 lengths add up to 16, and one of them is exactly 12.
All inputs are finite; a program needn't handle non-finite values.
Results may differ from a plain program's by a relative error of at most 0.014.
Values may be sent and summed in bfloat16 or wider, within the bound.
No kernel may reach another device: no remote copies, remote signals or barrier semaphores. Data moves between devices by JAX's collectives and lax.ppermute only.
A program may use at most 256 MiB of HBM per device.

v0:
```python
import jax
import jax.numpy as jnp
from jax import lax
from jax.sharding import PartitionSpec as P

HEAD = 128
WINDOW = 1024
BLOCK = 256


epsilon = 1e-06
negative = -1e30


def normalize(values, gain):
    factor = lax.rsqrt(jnp.mean(values * values, axis=-1, keepdims=True) + epsilon)
    scaled = values * factor
    return (scaled, factor, scaled * gain)


def norm_back(grad_norm, scaled, factor, gain):
    grad_scaled = grad_norm * gain
    inner = jnp.mean(grad_scaled * scaled, axis=-1, keepdims=True)
    return factor * (grad_scaled - scaled * inner)


def rotate(values, cosine, sine_table):
    half = values.shape[-1] // 2
    first = values[..., :half]
    second = values[..., half:]
    return jnp.concatenate(
        [first * cosine - second * sine_table, second * cosine + first * sine_table], axis=-1
    )


def unrotate(grads, cosine, sine_table):
    half = grads.shape[-1] // 2
    first = grads[..., :half]
    second = grads[..., half:]
    return jnp.concatenate(
        [first * cosine + second * sine_table, second * cosine - first * sine_table], axis=-1
    )


def matmul(left, right):
    return jnp.dot(left, right, preferred_element_type=jnp.float32)


def times_transposed(left, right):
    return lax.dot_general(
        left, right, (((1,), (1,)), ((), ())), preferred_element_type=jnp.float32
    )


def outer_sum(left, right):
    return lax.dot_general(
        left, right, (((0,), (0,)), ((), ())), preferred_element_type=jnp.float32
    )


def window_mask(block_number, start_block, spans):
    row_index = jnp.arange(BLOCK)[:, None]
    column_index = jnp.arange(spans * BLOCK)[None, :]
    reach = column_index // BLOCK
    distance = reach * BLOCK + row_index - column_index % BLOCK
    inside = (distance >= 0) & (distance < WINDOW)
    return inside & (block_number - reach >= start_block)


def per_device(
    block_input,
    cotangent,
    sequence_blocks,
    gain_attention,
    query_weight,
    keyval_weight,
    output_weight,
    gain_feedforward,
    gate_weight,
    up_weight,
    down_weight,
):
    count_dp = lax.axis_size("dp")
    device_dp = lax.axis_index("dp")
    device_tensor = lax.axis_index("tensor")
    rows_sub = block_input.shape[0]
    inputs_full, cotangent_full = (
        lax.all_gather(block_input, "tensor", axis=0, tiled=True),
        lax.all_gather(cotangent, "tensor", axis=0, tiled=True),
    )
    token_rows = inputs_full.shape[0]
    blocks_local = token_rows // BLOCK
    local_heads = query_weight.shape[1] // HEAD
    spans = WINDOW // BLOCK + 1
    scale = HEAD ** (-0.5)
    own_start = device_tensor * rows_sub
    ends = jnp.cumsum(sequence_blocks)
    block_numbers = jnp.arange(blocks_local, dtype=jnp.int32) * count_dp + device_dp
    starts = jnp.sum(
        jnp.where(ends[None, :] <= block_numbers[:, None], sequence_blocks[None, :], 0), axis=1
    )
    positions = (
        ((block_numbers - starts)[:, None] * BLOCK + jnp.arange(BLOCK, dtype=jnp.int32)[None, :])
        .reshape(token_rows)
        .astype(jnp.float32)
    )
    frequency = 10000.0 ** (-jnp.arange(HEAD // 2, dtype=jnp.float32) * 2.0 / HEAD)
    angles = positions[:, None] * frequency[None, :]
    cosine = jnp.cos(angles)
    sine_table = jnp.sin(angles)
    inputs_float = inputs_full.astype(jnp.float32)
    scaled_one, factor_one, normed_one = normalize(inputs_float, gain_attention)
    normed_low = normed_one.astype(jnp.bfloat16)
    query_raw = matmul(normed_low, query_weight).reshape(token_rows, local_heads, HEAD)
    queries = rotate(query_raw, cosine[:, None, :], sine_table[:, None, :]).astype(jnp.bfloat16)
    keyval_raw = matmul(normed_low, keyval_weight)
    keys_own = (
        rotate(keyval_raw[:, :HEAD], cosine, sine_table)
        .astype(jnp.bfloat16)
        .reshape(blocks_local, BLOCK, HEAD)
    )
    values_own = keyval_raw[:, HEAD:].astype(jnp.bfloat16).reshape(blocks_local, BLOCK, HEAD)
    sources = jnp.maximum(
        block_numbers[:, None] - jnp.arange(1, spans, dtype=jnp.int32)[None, :], 0
    )
    places = sources % count_dp * blocks_local + sources // count_dp
    every_keys, every_values = (
        lax.all_gather(keys_own, "dp", axis=0, tiled=True),
        lax.all_gather(values_own, "dp", axis=0, tiled=True),
    )
    near_keys = every_keys[places]
    near_values = every_values[places]
    window_keys = jnp.concatenate([keys_own[:, None], near_keys], axis=1).reshape(
        blocks_local, spans * BLOCK, HEAD
    )
    window_values = jnp.concatenate([values_own[:, None], near_values], axis=1).reshape(
        blocks_local, spans * BLOCK, HEAD
    )
    query_blocks = queries.reshape(blocks_local, BLOCK, local_heads, HEAD).transpose(0, 2, 1, 3)
    masks = []
    attended_list = []
    log_totals = []
    for slot in range(blocks_local):
        allowed = window_mask(block_numbers[slot], starts[slot], spans)
        masks.append(allowed)
        scores = (
            jnp.einsum(
                "hqd,kd->hqk",
                query_blocks[slot],
                window_keys[slot],
                preferred_element_type=jnp.float32,
            )
            * scale
        )
        scores = jnp.where(allowed[None], scores, negative)
        peak = jnp.max(scores, axis=-1, keepdims=True)
        exponent = jnp.exp(scores - peak)
        total = jnp.sum(exponent, axis=-1, keepdims=True)
        weights_soft = exponent / total
        log_totals.append(peak + jnp.log(total))
        attended_list.append(
            jnp.einsum(
                "hqk,kd->hqd",
                weights_soft.astype(jnp.bfloat16),
                window_values[slot],
                preferred_element_type=jnp.float32,
            )
        )
    attended = (
        jnp.stack(attended_list, axis=0)
        .transpose(0, 2, 1, 3)
        .reshape(token_rows, local_heads * HEAD)
    )
    attended_low = attended.astype(jnp.bfloat16)
    attention_part = times_transposed(attended_low, output_weight)
    attention_total = lax.psum(attention_part, "tensor")
    hidden_state = inputs_float + attention_total
    scaled_two, factor_two, normed_two = normalize(hidden_state, gain_feedforward)
    normed_two_low = normed_two.astype(jnp.bfloat16)
    own_hidden = lax.dynamic_slice_in_dim(hidden_state, own_start, rows_sub, 0)
    gate = matmul(normed_two_low, gate_weight)
    upper = matmul(normed_two_low, up_weight)
    activated, gelu_back = jax.vjp(lambda value: jax.nn.gelu(value, approximate=True), gate)
    product_low = (activated * upper).astype(jnp.bfloat16)
    feed_rows = lax.psum_scatter(
        times_transposed(product_low, down_weight).astype(jnp.bfloat16),
        "tensor",
        scatter_dimension=0,
        tiled=True,
    ).astype(jnp.float32)
    block_output = (own_hidden + feed_rows).astype(jnp.bfloat16)
    grad_product = matmul(cotangent_full, down_weight)
    grad_down = outer_sum(cotangent_full, product_low)
    grad_gate_raw = gelu_back(grad_product * upper)[0]
    grad_gate_low = grad_gate_raw.astype(jnp.bfloat16)
    grad_up_low = (grad_product * activated).astype(jnp.bfloat16)
    grad_gate_weight = outer_sum(normed_two_low, grad_gate_low)
    grad_up_weight = outer_sum(normed_two_low, grad_up_low)
    grad_norm_two_part = times_transposed(grad_gate_low, gate_weight) + times_transposed(
        grad_up_low, up_weight
    )
    grad_norm_two = lax.psum(grad_norm_two_part, "tensor")
    grad_hidden = cotangent_full.astype(jnp.float32) + norm_back(
        grad_norm_two, scaled_two, factor_two, gain_feedforward
    )
    grad_attention_low = grad_hidden.astype(jnp.bfloat16)
    own_grad_hidden = lax.dynamic_slice_in_dim(grad_hidden, own_start, rows_sub, 0)
    own_grad_norm_two = lax.dynamic_slice_in_dim(grad_norm_two, own_start, rows_sub, 0)
    own_scaled_two = lax.dynamic_slice_in_dim(scaled_two, own_start, rows_sub, 0)
    gain_two_part = jnp.sum(own_grad_norm_two * own_scaled_two, axis=0)
    grad_output_weight = outer_sum(grad_attention_low, attended_low)
    grad_attended = matmul(grad_attention_low, output_weight).astype(jnp.bfloat16)
    grad_attended_blocks = grad_attended.reshape(blocks_local, BLOCK, local_heads, HEAD).transpose(
        0, 2, 1, 3
    )
    grad_query_list = []
    grad_key_list = []
    grad_value_list = []
    for slot in range(blocks_local):
        scores = (
            jnp.einsum(
                "hqd,kd->hqk",
                query_blocks[slot],
                window_keys[slot],
                preferred_element_type=jnp.float32,
            )
            * scale
        )
        scores = jnp.where(masks[slot][None], scores, negative)
        weights_soft = jnp.exp(scores - log_totals[slot])
        grad_weights = jnp.einsum(
            "hqd,kd->hqk",
            grad_attended_blocks[slot],
            window_values[slot],
            preferred_element_type=jnp.float32,
        )
        grad_scores = weights_soft * (
            grad_weights - jnp.sum(grad_weights * weights_soft, axis=-1, keepdims=True)
        )
        grad_scores_low = grad_scores.astype(jnp.bfloat16)
        grad_query_list.append(
            jnp.einsum(
                "hqk,kd->hqd",
                grad_scores_low,
                window_keys[slot],
                preferred_element_type=jnp.float32,
            )
            * scale
        )
        grad_key_list.append(
            jnp.einsum(
                "hqk,hqd->kd",
                grad_scores_low,
                query_blocks[slot],
                preferred_element_type=jnp.float32,
            )
            * scale
        )
        grad_value_list.append(
            jnp.einsum(
                "hqk,hqd->kd",
                weights_soft.astype(jnp.bfloat16),
                grad_attended_blocks[slot],
                preferred_element_type=jnp.float32,
            )
        )
    grad_window_keys = jnp.stack(grad_key_list, axis=0).reshape(blocks_local, spans, BLOCK, HEAD)
    grad_window_values = jnp.stack(grad_value_list, axis=0).reshape(
        blocks_local, spans, BLOCK, HEAD
    )
    remote_keys = grad_window_keys[:, 1:]
    remote_values = grad_window_values[:, 1:]
    empty = jnp.zeros((count_dp * blocks_local, BLOCK, HEAD), jnp.float32)
    flat_places = places.reshape(-1)
    buffer_keys = empty.at[flat_places].add(remote_keys.reshape(-1, BLOCK, HEAD))
    buffer_values = empty.at[flat_places].add(remote_values.reshape(-1, BLOCK, HEAD))
    back_keys, back_values = (
        lax.psum_scatter(buffer_keys, "dp", scatter_dimension=0, tiled=True),
        lax.psum_scatter(buffer_values, "dp", scatter_dimension=0, tiled=True),
    )
    total_keys = (grad_window_keys[:, 0] + back_keys).reshape(token_rows, HEAD)
    total_values = (grad_window_values[:, 0] + back_values).reshape(token_rows, HEAD)
    grad_query_rotated = (
        jnp.stack(grad_query_list, axis=0)
        .transpose(0, 2, 1, 3)
        .reshape(token_rows, local_heads, HEAD)
    )
    grad_query_low = (
        unrotate(grad_query_rotated, cosine[:, None, :], sine_table[:, None, :])
        .reshape(token_rows, local_heads * HEAD)
        .astype(jnp.bfloat16)
    )
    grad_query_weight = outer_sum(normed_low, grad_query_low)
    grad_norm_one_part = times_transposed(grad_query_low, query_weight)
    norm_one_sum, keys_sum, values_sum, grad_gain_two = lax.psum(
        (grad_norm_one_part, total_keys, total_values, gain_two_part), "tensor"
    )
    grad_key_low = unrotate(keys_sum, cosine, sine_table).astype(jnp.bfloat16)
    grad_value_low = values_sum.astype(jnp.bfloat16)
    grad_keyval_low = jnp.concatenate([grad_key_low, grad_value_low], axis=1)
    grad_keyval_weight = outer_sum(normed_low, grad_keyval_low)
    grad_norm_one = norm_one_sum + times_transposed(grad_keyval_low, keyval_weight)
    grad_gain_one = jnp.sum(grad_norm_one * scaled_one, axis=0)
    own_grad_norm_one = lax.dynamic_slice_in_dim(grad_norm_one, own_start, rows_sub, 0)
    own_scaled_one = lax.dynamic_slice_in_dim(scaled_one, own_start, rows_sub, 0)
    own_factor_one = lax.dynamic_slice_in_dim(factor_one, own_start, rows_sub, 0)
    grad_rows = own_grad_hidden + norm_back(
        own_grad_norm_one, own_scaled_one, own_factor_one, gain_attention
    )
    summed = (
        lax.psum_scatter(grad_gain_one, "dp", scatter_dimension=0, tiled=True),
        lax.psum_scatter(grad_query_weight, "dp", scatter_dimension=0, tiled=True),
        lax.psum_scatter(grad_keyval_weight, "dp", scatter_dimension=0, tiled=True),
        lax.psum_scatter(grad_output_weight, "dp", scatter_dimension=0, tiled=True),
        lax.psum_scatter(grad_gain_two, "dp", scatter_dimension=0, tiled=True),
        lax.psum_scatter(grad_gate_weight, "dp", scatter_dimension=0, tiled=True),
        lax.psum_scatter(grad_up_weight, "dp", scatter_dimension=0, tiled=True),
        lax.psum_scatter(grad_down, "dp", scatter_dimension=0, tiled=True),
    )
    return (
        block_output,
        grad_rows,
        summed[0],
        summed[1],
        summed[2],
        summed[3],
        summed[4],
        summed[5],
        summed[6],
        summed[7],
    )


def solution(mesh):
    placed = (
        P(("dp", "tensor"), None),
        P(("dp", "tensor"), None),
        P(),
        P(),
        P(None, "tensor"),
        P(),
        P(None, "tensor"),
        P(),
        P(None, "tensor"),
        P(None, "tensor"),
        P(None, "tensor"),
    )
    return jax.shard_map(
        per_device,
        mesh=mesh,
        in_specs=placed,
        out_specs=(
            P(("dp", "tensor"), None),
            P(("dp", "tensor"), None),
            P("dp"),
            P("dp", "tensor"),
            P("dp", None),
            P("dp", "tensor"),
            P("dp"),
            P("dp", "tensor"),
            P("dp", "tensor"),
            P("dp", "tensor"),
        ),
        check_vma=False,
    )
```

profile of v0, /device:TPU:0, one launch (start us, length us, event | category | flops | bytes accessed | tf_op | source)
XLA Modules:
  0.0 1557.8 jit_solution(17093098948610843244)
XLA Ops:
  8.0 26.9 %all-gather.5.cloned.1.call-done = bf16[512,2048]{1,0:T(8,128)(2,1)} async-done(((bf16[128,2048]{1,0:T(8,128)(2,1)}), bf16[512,2048]{1,0:T(8,128)(2,1)}) %all-gather.5.cloned.1.call-update) | async-done | bytes 2097168 | tf_op jit(solution)/shard_map/all_gather | solution.py:88
  63.3 18.2 %all-gather.9.cloned.1.call-done = bf16[16,256,128]{2,1,0:T(8,128)(2,1)} async-done(((bf16[2,256,128]{2,1,0:T(8,128)(2,1)}), bf16[16,256,128]{2,1,0:T(8,128)(2,1)}) %all-gather.9.cloned.1.call-update) | async-done | bytes 1048592 | tf_op jit(solution)/shard_map/all_gather | solution.py:129
  86.1 36.4 %all-gather.7.cloned.1.call-done = bf16[16,256,128]{2,1,0:T(8,128)(2,1)} async-done(((bf16[2,256,128]{2,1,0:T(8,128)(2,1)}), bf16[16,256,128]{2,1,0:T(8,128)(2,1)}) %all-gather.7.cloned.1.call-update) | async-done | bytes 1048592 | tf_op jit(solution)/shard_map/all_gather | solution.py:128
  141.7 83.5 %all-reduce.9.cloned.1.call-done = f32[512,2048]{1,0:T(8,128)} async-done(((f32[512,2048]{1,0:T(8,128)}), f32[512,2048]{1,0:T(8,128)}) %all-reduce.9.cloned.1.call-update) | async-done | bytes 4194320 | tf_op jit(solution)/shard_map/psum | solution.py:176
  232.9 9.0 fusion.112
  241.9 5.2 fusion.111
  249.5 11.8 multiply_convert_fusion.4
  261.2 6.7 fusion.113
  267.9 7.8 convolution_add_fusion.1
  276.7 84.8 %all-reduce.11.cloned.1.call-done = f32[512,2048]{1,0:T(8,128)} async-done(((f32[512,2048]{1,0:T(8,128)}), f32[512,2048]{1,0:T(8,128)}) %all-reduce.11.cloned.1.call-update) | async-done | bytes 4194320 | tf_op jit(solution)/shard_map/psum | solution.py:202
  382.8 4.8 multiply_convert_fusion
  395.8 6.7 fusion.2
  428.7 5.0 fusion.114
  433.7 29.6 %reduce-scatter.12.cloned.1.call-done = f32[2,256,128]{2,1,0:T(8,128)} async-done(((f32[16,256,128]{2,1,0:T(8,128)}), f32[2,256,128]{2,1,0:T(8,128)}) %reduce-scatter.12.cloned.1.call-update) | async-done | bytes 262160 | tf_op jit(solution)/shard_map/reduce_scatter | solution.py:278
  465.1 8.2 convolution_convert_fusion
  473.3 7.9 convolution_bitcast_fusion
  482.3 5.5 fusion.34
  493.1 40.7 %reduce-scatter.14.cloned.1.call-done = f32[2,256,128]{2,1,0:T(8,128)} async-done(((f32[16,256,128]{2,1,0:T(8,128)}), f32[2,256,128]{2,1,0:T(8,128)}) %reduce-scatter.14.cloned.1.call-update) | async-done | bytes 262160 | tf_op jit(solution)/shard_map/reduce_scatter | solution.py:279
  535.4 16.6 %all-reduce.14 = bf16[512,128]{1,0:T(8,128)(2,1)S(1)} all-reduce(f32[512,128]{1,0:T(8,128)} %bitcast.231), channel_id=1, replica_groups=mesh['dp'=8,'tensor'=4] {'tensor'}, use_global_device_ids=true, to_apply=%region_20.21 | all-reduce | flops 65536 | bytes 393216 | tf_op jit(solution)/shard_map/psum | solution.py:295
  552.1 75.8 %all-reduce.13.cloned.1.call-done = (f32[512,2048]{1,0:T(8,128)}, f32[512,128]{1,0:T(8,128)}) async-done(((f32[512,2048]{1,0:T(8,128)}, f32[512,128]{1,0:T(8,128)}), (f32[512,2048]{1,0:T(8,128)}, f32[512,128]{1,0:T(8,128)})) %all-reduce.13.cloned.1.call-update) | async-done | bytes 4456464 | tf_op jit(solution)/shard_map/psum | solution.py:295
  632.5 10.1 fusion.116
  642.9 10.0 fusion.115
  657.1 4.7 reduce-scatter.10.cloned.1.call-done
  664.1 7.1 multiply_reduce_fusion.2
  671.2 38.8 %all-reduce.2 = (f32[2048]{0:T(1024)S(1)}, f32[2048]{0:T(1024)S(1)}) all-reduce(f32[2048]{0:T(1024)} %get-tuple-element.73, f32[2048]{0:T(1024)S(1)} %multiply_reduce_fusion.5), channel_id=5, replica_groups=mesh['dp'=8,'tensor'=4] {'dp'}, use_global_device_ids=true, to_apply=%region_23.24.clone | all-reduce | flops 4096 | bytes 32768
  710.7 6.6 psum.48
  722.4 151.6 %reduce-scatter.26.cloned.1.call-done = f32[256,1536]{0,1:T(8,128)} async-done(((f32[2048,1536]{0,1:T(8,128)}), f32[256,1536]{0,1:T(8,128)}) %reduce-scatter.26.cloned.1.call-update) | async-done | bytes 1572880 | tf_op jit(solution)/shard_map/reduce_scatter | solution.py:318
  877.0 88.5 %reduce-scatter.20.cloned.1.call-done = f32[256,512]{1,0:T(8,128)} async-done(((f32[2048,512]{1,0:T(8,128)}), f32[256,512]{1,0:T(8,128)}) %reduce-scatter.20.cloned.1.call-update) | async-done | bytes 524304 | tf_op jit(solution)/shard_map/reduce_scatter | solution.py:314
  965.6 91.9 %reduce-scatter.16.cloned.1.call-done = f32[256,512]{1,0:T(8,128)} async-done(((f32[2048,512]{1,0:T(8,128)}), f32[256,512]{1,0:T(8,128)}) %reduce-scatter.16.cloned.1.call-update) | async-done | bytes 524304 | tf_op jit(solution)/shard_map/reduce_scatter | solution.py:312
  1057.5 72.0 %reduce-scatter.18.cloned.1.call-done = f32[256,256]{1,0:T(8,128)} async-done(((f32[2048,256]{1,0:T(8,128)}), f32[256,256]{1,0:T(8,128)}) %reduce-scatter.18.cloned.1.call-update) | async-done | bytes 262160 | tf_op jit(solution)/shard_map/reduce_scatter | solution.py:313
  1129.5 210.7 %reduce-scatter.24.cloned.1.call-done = f32[256,1536]{1,0:T(8,128)} async-done(((f32[2048,1536]{1,0:T(8,128)}), f32[256,1536]{1,0:T(8,128)}) %reduce-scatter.24.cloned.1.call-update) | async-done | bytes 1572880 | tf_op jit(solution)/shard_map/reduce_scatter | solution.py:317
  1340.2 210.8 %reduce-scatter.22.cloned.1.call-done = f32[256,1536]{1,0:T(8,128)} async-done(((f32[2048,1536]{1,0:T(8,128)}), f32[256,1536]{1,0:T(8,128)}) %reduce-scatter.22.cloned.1.call-update) | async-done | bytes 1572880 | tf_op jit(solution)/shard_map/reduce_scatter | solution.py:316
  (255 shorter events, 148.1 us)
Async XLA Ops:
  7.2 130.4 %copy-start = (bf16[2048,512]{1,0:T(8,128)(2,1)S(1)}, bf16[2048,512]{1,0:T(8,128)(2,1)}, u32[]{:S(2)}) copy-start(bf16[2048,512]{1,0:T(8,128)(2,1)} %param.17) | copy-start | bytes 6291460
  7.2 27.7 %all-gather.5.cloned.1.call-start = ((), (), s32[]{:S(2)}) async-start(), calls=%async_computation.9 | async-start | bytes 2621440 | tf_op jit(solution)/shard_map/all_gather | solution.py:88
  7.9 33.4 %copy-start.50 = (s32[2]{0:T(128)S(1)}, s32[2]{0:T(128)}, u32[]{:S(2)}) copy-start(s32[2]{0:T(128)} %param.13) | copy-start | bytes 28
  7.9 73.5 %all-gather.9.cloned.1.call-start = ((), (), s32[]{:S(2)}) async-start(), calls=%async_computation.11 | async-start | bytes 1179648 | tf_op jit(solution)/shard_map/all_gather | solution.py:129
  37.0 12.9 copy-start.45
  37.0 12.9 copy-start.42
  41.2 81.4 %all-gather.7.cloned.1.call-start = ((), (), s32[]{:S(2)}) async-start(), calls=%async_computation.10 | async-start | bytes 1179648 | tf_op jit(solution)/shard_map/all_gather | solution.py:128
  41.8 11.8 copy-start.47
  47.9 13.2 copy-start.29
  47.9 13.2 copy-start.31
  49.3 175.9 %all-reduce.9.cloned.1.call-start = ((), (), s32[]{:S(2)}) async-start(), calls=%async_computation.12 | async-start | bytes 8388608 | tf_op jit(solution)/shard_map/psum | solution.py:176
  49.9 79.9 %copy-start.13 = (pred[256,1280]{1,0:T(8,128)(4,1)}, pred[256,1280]{1,0:T(8,128)(4,1)S(1)}, u32[]{:S(2)}) copy-start(pred[256,1280]{1,0:T(8,128)(4,1)S(1)} %get-tuple-element.90) | copy-start | bytes 983044
  61.1 64.0 %copy-start.41 = (bf16[2,1,256,128]{3,2,1,0:T(8,128)(2,1)S(1)}, bf16[2,1,256,128]{3,2,1,0:T(8,128)(2,1)}, u32[]{:S(2)}) copy-start(bf16[2,1,256,128]{3,2,1,0:T(8,128)(2,1)} %maximum_bitcast_fusion.4) | copy-start | bytes 393220
  63.3 68.4 %copy-start.25 = (bf16[2,4,256,128]{3,2,1,0:T(8,128)(2,1)}, bf16[2,4,256,128]{3,2,1,0:T(8,128)(2,1)S(1)}, u32[]{:S(2)}) copy-start(bf16[2,4,256,128]{3,2,1,0:T(8,128)(2,1)S(1)} %copy_bitcast_fusion) | copy-start | bytes 1572868
  140.8 108.6 %all-gather.11.cloned.1.call-start = ((), (), s32[]{:S(2)}) async-start(), calls=%async_computation.14 | async-start | bytes 2621440 | tf_op jit(solution)/shard_map/all_gather | solution.py:89
  141.4 87.3 %copy-start.44 = (f32[2048]{0:T(1024)S(1)}, f32[2048]{0:T(1024)}, u32[]{:S(2)}) copy-start(f32[2048]{0:T(1024)} %param.18) | copy-start | bytes 24580
  141.4 220.0 %all-reduce.11.cloned.1.call-start = ((), (), s32[]{:S(2)}) async-start(), calls=%async_computation.15 | async-start | bytes 8388608 | tf_op jit(solution)/shard_map/psum | solution.py:202
  228.7 13.2 slice-start.4
  275.8 187.5 %reduce-scatter.12.cloned.1.call-start = ((), (), s32[]{:S(2)}) async-start(), calls=%async_computation.16 | async-start | bytes 2359296 | tf_op jit(solution)/shard_map/reduce_scatter | solution.py:278
  395.1 138.7 %reduce-scatter.14.cloned.1.call-start = ((), (), s32[]{:S(2)}) async-start(), calls=%async_computation.17 | async-start | bytes 2359296 | tf_op jit(solution)/shard_map/reduce_scatter | solution.py:279
  422.2 205.7 %all-reduce.13.cloned.1.call-start = ((), (), s32[]{:S(2)}) async-start(), calls=%async_computation.24 | async-start | bytes 8912896 | tf_op jit(solution)/shard_map/psum | solution.py:295
  465.0 196.8 %reduce-scatter.10.cloned.1.call-start = ((), (), s32[]{:S(2)}) async-start(), calls=%async_computation.13 | async-start | bytes 2621440 | tf_op jit(solution)/shard_map/reduce_scatter | solution.py:185
  473.3 400.7 %reduce-scatter.26.cloned.1.call-start = ((), (), s32[]{:S(2)}) async-start(), calls=%async_computation.23 | async-start | bytes 14155776 | tf_op jit(solution)/shard_map/reduce_scatter | solution.py:318
  481.2 484.3 %reduce-scatter.20.cloned.1.call-start = ((), (), s32[]{:S(2)}) async-start(), calls=%async_computation.20 | async-start | bytes 4718592 | tf_op jit(solution)/shard_map/reduce_scatter | solution.py:314
  487.8 569.6 %reduce-scatter.16.cloned.1.call-start = ((), (), s32[]{:S(2)}) async-start(), calls=%async_computation.18 | async-start | bytes 4718592 | tf_op jit(solution)/shard_map/reduce_scatter | solution.py:312
  493.0 40.8 %copy-start.20 = (f32[1,5,256,128]{3,2,1,0:T(8,128)S(1)}, f32[1,5,256,128]{3,2,1,0:T(8,128)}, u32[]{:S(2)}) copy-start(f32[1,5,256,128]{3,2,1,0:T(8,128)} %copy-done.19) | copy-start | bytes 1966084
  493.0 40.8 %copy-start.22 = (f32[1,5,256,128]{3,2,1,0:T(8,128)S(1)}, f32[1,5,256,128]{3,2,1,0:T(8,128)}, u32[]{:S(2)}) copy-start(f32[1,5,256,128]{3,2,1,0:T(8,128)} %copy-done.21) | copy-start | bytes 1966084
  493.0 134.9 %copy-start.48 = (f32[1,2,2,128]{3,1,2,0:T(2,128)S(1)}, f32[1,2,2,128]{3,1,2,0:T(2,128)}, u32[]{:S(2)}) copy-start(f32[1,2,2,128]{3,1,2,0:T(2,128)} %copy-done.47) | copy-start | bytes 6148
  493.0 636.5 %reduce-scatter.18.cloned.1.call-start = ((), (), s32[]{:S(2)}) async-start(), calls=%async_computation.19 | async-start | bytes 2359296 | tf_op jit(solution)/shard_map/reduce_scatter | solution.py:313
  632.5 707.7 %reduce-scatter.24.cloned.1.call-start = ((), (), s32[]{:S(2)}) async-start(), calls=%async_computation.22 | async-start | bytes 14155776 | tf_op jit(solution)/shard_map/reduce_scatter | solution.py:317
  642.6 908.3 %reduce-scatter.22.cloned.1.call-start = ((), (), s32[]{:S(2)}) async-start(), calls=%async_computation.21 | async-start | bytes 14155776 | tf_op jit(solution)/shard_map/reduce_scatter | solution.py:316
  717.3 833.6 %copy-start.1 = (bf16[2048,512]{1,0:T(8,128)(2,1)S(1)}, bf16[2048,512]{1,0:T(8,128)(2,1)}, u32[]{:S(2)}) copy-start(bf16[2048,512]{1,0:T(8,128)(2,1)} %param.17) | copy-start | bytes 6291460
  (44 other events, 177.1 us)
Sparse Core Ops, SparseCore 0:
  9.6 25.2 all-gather.4
  41.3 40.1 all-gather.8
  83.6 38.8 all-gather.6
  141.0 84.2 all-reduce.8
  226.7 22.7 all-gather.10
  275.9 85.4 all-reduce.10
  395.2 68.0 reduce-scatter.11
  466.8 66.8 reduce-scatter.13
  536.8 91.0 all-reduce.12
  630.2 31.5 reduce-scatter.9
  665.9 208.1 reduce-scatter.25
  878.5 86.9 reduce-scatter.19
  969.8 87.6 reduce-scatter.15
  1061.8 67.6 reduce-scatter.17
  1133.9 206.2 reduce-scatter.23
  1344.6 206.3 reduce-scatter.21
where the time goes:
time: 1570 us; the launch traced here: 1560 us
  waiting for transfers between devices  1230 us (78%)
  matrix products  138 us (9%)
  other arithmetic  65.2 us (4%)
  blocking collectives  62 us (4%)
  local copies, waits for them, and re-layouts  45 us (3%)
  between operations  15.8 us (1%)
    reduce_scatter x1, waiting for transfers between devices, per_device(): lax.psum_scatter(grad_gate_weight, 'dp', scatter_dimension=0, tiled=True)  211 us
    reduce_scatter x1, waiting for transfers between devices, per_device(): lax.psum_scatter(grad_up_weight, 'dp', scatter_dimension=0, tiled=True)  211 us
    reduce_scatter x1, waiting for transfers between devices, per_device(): lax.psum_scatter(grad_down, 'dp', scatter_dimension=0, tiled=True)  152 us
    reduce_scatter x1, waiting for transfers between devices, per_device(): lax.psum_scatter(grad_query_weight, 'dp', scatter_dimension=0, tiled=True)  91.9 us
    reduce_scatter x1, waiting for transfers between devices, per_device(): lax.psum_scatter(grad_output_weight, 'dp', scatter_dimension=0, tiled=True)  88.5 us
    psum x1, waiting for transfers between devices, per_device(): grad_norm_two = lax.psum(grad_norm_two_part, 'tensor')  84.8 us
    psum x1, waiting for transfers between devices, per_device(): attention_total = lax.psum(attention_part, 'tensor')  83.5 us
    psum x1, waiting for transfers between devices, per_device(): lax.psum((grad_norm_one_part, total_keys, total_values, gain_two_part), '...  75.8 us
  transfers between devices with their start and end apart: 16, of which 16 were waited for; matrix products, arithmetic and copies ran while one was open for 10% of the time, Pallas kernels for 0%

commit v1 on v0

v1 whole, which is shorter than its diff:
```python
import jax
import jax.numpy as jnp
from jax import lax
from jax.sharding import PartitionSpec as P

HEAD = 128
WINDOW = 1024
BLOCK = 256
SPANS = WINDOW // BLOCK + 1

epsilon = 1e-06
negative = -1e30
low_type = jnp.bfloat16


def matmul(left, right):
    return jnp.dot(left, right, preferred_element_type=jnp.float32)


def times_transposed(left, right):
    return lax.dot_general(
        left, right, (((1,), (1,)), ((), ())), preferred_element_type=jnp.float32
    )


def outer_sum(left, right):
    return lax.dot_general(
        left, right, (((0,), (0,)), ((), ())), preferred_element_type=jnp.float32
    )


def flip(value, axis, bit):
    count = lax.axis_size(axis)
    return lax.ppermute(value, axis, [(i, i ^ bit) for i in range(count)])


def shift(value, step):
    count = lax.axis_size("dp")
    return lax.ppermute(value, "dp", [(i, (i + step) % count) for i in range(count)])


def gather_tensor(value):
    over = flip(value, "tensor", 2)
    return [value, flip(value, "tensor", 1), over, flip(over, "tensor", 1)]


def scatter_tensor(front, back):
    rows = front.shape[0] // 2
    far = back[:rows] + flip(back[rows:].astype(low_type), "tensor", 1)
    near = front[:rows] + flip(front[rows:].astype(low_type), "tensor", 1)
    return near + flip(far.astype(low_type), "tensor", 2)


def bit_of(index, bit):
    return (index >> bit) & 1


def pick(value, axis, index):
    return lax.dynamic_index_in_dim(value, index, axis, keepdims=False)


def reduce_weight(pairs, order, dp):
    count = lax.axis_size("dp")
    bits = sorted(order, reverse=True)
    lefts = []
    for left, _ in pairs:
        lefts.append(left.reshape(left.shape[0], *([2] * len(bits)), -1))
    rights = [right for _, right in pairs]
    size = lefts[0].shape[-1]
    width = rights[0].shape[1]
    pending = []

    def product(chosen, waiting):
        total = None
        for left, right in zip(chosen, rights):
            part = outer_sum(left.reshape(left.shape[0], -1), right)
            total = part if total is None else total + part
        for item in waiting:
            total = total + item.reshape(total.shape).astype(jnp.float32)
        return total

    for bit in order:
        place = bits.index(bit)
        mine = bit_of(dp, bit)
        away = product(
            [pick(left, place + 1, 1 - mine) for left in lefts],
            [pick(item, place, 1 - mine) for item in pending],
        ).astype(low_type)
        arrived = flip(away, "dp", 1 << bit)
        bits.remove(bit)
        lefts = [pick(left, place + 1, mine) for left in lefts]
        pending = [pick(item, place, mine) for item in pending]
        pending.append(arrived.reshape(*([2] * len(bits)), size, width))
    return product(lefts, pending)


def rotate(values, cosine, sine):
    half = values.shape[-1] // 2
    first = values[..., :half]
    second = values[..., half:]
    return jnp.concatenate(
        [first * cosine - second * sine, second * cosine + first * sine], axis=-1
    )


def gelu_parts(gate):
    root = 0.7978845608028654
    square = gate * gate
    curve = jnp.tanh(root * gate * (1.0 + 0.044715 * square))
    half = 0.5 * (1.0 + curve)
    slope = half + 0.5 * gate * (1.0 - curve * curve) * root * (1.0 + 3 * 0.044715 * square)
    return gate * half, slope


def per_device(
    block_input,
    cotangent,
    sequence_blocks,
    gain_attention,
    query_weight,
    keyval_weight,
    output_weight,
    gain_feedforward,
    gate_weight,
    up_weight,
    down_weight,
):
    count = lax.axis_size("dp")
    bits = count.bit_length() - 1
    dp = lax.axis_index("dp")
    rank = lax.axis_index("tensor")
    slot = rank >> 1
    side = rank & 1
    rows = block_input.shape[0]
    width = block_input.shape[1]
    heads = query_weight.shape[1] // HEAD
    scale = HEAD ** (-0.5)
    top = bits - 1
    half_width = width // 2
    half_start = bit_of(dp, top) * half_width

    def positions_of(number, offsets):
        ends = jnp.sum(
            jnp.where(
                jnp.arange(sequence_blocks.shape[0])[:, None]
                >= jnp.arange(sequence_blocks.shape[0])[None, :],
                sequence_blocks[None, :],
                0,
            ),
            axis=1,
        )
        start = jnp.sum(jnp.where(ends <= number, sequence_blocks, 0))
        return start, ((number - start) * BLOCK + offsets).astype(jnp.float32)

    def tables(position):
        frequency = 10000.0 ** (-jnp.arange(HEAD // 2, dtype=jnp.float32) * 2.0 / HEAD)
        angles = position[:, None] * frequency[None, :]
        return jnp.cos(angles), jnp.sin(angles)

    place = jnp.arange(rows, dtype=jnp.int32)
    both_sides = jnp.concatenate([side * rows + place, (1 - side) * rows + place])
    numbers = [dp + slot * count, dp + (1 - slot) * count]
    starts, cosines, sines = [], [], []
    for number in numbers:
        start, position = positions_of(number, both_sides)
        cosine, sine = tables(position)
        starts.append(start)
        cosines.append(cosine)
        sines.append(sine)
    own_cosine, own_sine = cosines[0][:rows], sines[0][:rows]
    cosine_all = jnp.concatenate(cosines)
    sine_all = jnp.concatenate(sines)

    own_input = block_input.astype(jnp.float32)
    factor_one = lax.rsqrt(jnp.mean(own_input * own_input, axis=-1, keepdims=True) + epsilon)
    scaled_one = own_input * factor_one
    own_normed = (scaled_one * gain_attention).astype(low_type)

    keyval = matmul(own_normed, keyval_weight)
    own_keyval = jnp.concatenate(
        [rotate(keyval[:, :HEAD], own_cosine, own_sine), keyval[:, HEAD:]], axis=1
    ).astype(low_type)
    near = [own_keyval] + [shift(own_keyval, k) for k in range(1, SPANS)]
    keyvals = gather_tensor(jnp.stack(near))
    keyvals = jnp.stack(
        [jnp.stack(keyvals[:2], axis=1), jnp.stack(keyvals[2:], axis=1)]
    )

    normed = jnp.concatenate(gather_tensor(own_normed))
    query_raw = matmul(normed, query_weight).reshape(4 * rows, heads, HEAD)
    queries = rotate(query_raw, cosine_all[:, None, :], sine_all[:, None, :]).astype(low_type)

    cotangent_far = flip(cotangent, "dp", 1 << top)
    cotangents = [
        jnp.concatenate(gather_tensor(cotangent)),
        jnp.concatenate(gather_tensor(cotangent_far)),
    ]

    sources = []
    windows = []
    allowed = []
    logs = []
    attended = []
    query_blocks = [
        queries[: 2 * rows].transpose(1, 0, 2),
        queries[2 * rows :].transpose(1, 0, 2),
    ]
    for u in range(2):
        is_late = (slot ^ u) == 1
        from_late = [is_late & (dp >= k) for k in range(SPANS)]
        from_other = [(late != (slot == 1)) for late in from_late]
        sources.append(from_other)
        window = jnp.concatenate(
            [
                jnp.where(from_other[k], keyvals[1, k], keyvals[0, k]).reshape(BLOCK, 2 * HEAD)
                for k in range(SPANS)
            ]
        )
        windows.append((window[:, :HEAD], window[:, HEAD:]))
        reach = jnp.repeat(jnp.arange(SPANS, dtype=jnp.int32), BLOCK)
        key_offset = reach * BLOCK - jnp.tile(both_sides, SPANS)
        distance = both_sides[:, None] + key_offset[None, :]
        mask = (distance >= 0) & (distance < WINDOW)
        mask = mask & ((numbers[u] - reach) >= starts[u])[None, :]
        allowed.append(mask)
        scores = (
            jnp.einsum(
                "hqd,kd->hqk",
                query_blocks[u],
                windows[u][0],
                preferred_element_type=jnp.float32,
            )
            * scale
        )
        scores = jnp.where(mask[None], scores, negative)
        peak = jnp.max(scores, axis=-1, keepdims=True)
        exponent = jnp.exp(scores - peak)
        total = jnp.sum(exponent, axis=-1, keepdims=True)
        soft = (exponent / total).astype(low_type)
        logs.append(peak + jnp.log(total))
        attended.append(
            jnp.einsum(
                "hqk,kd->hqd", soft, windows[u][1], preferred_element_type=jnp.float32
            )
            .transpose(1, 0, 2)
            .reshape(2 * rows, heads * HEAD)
            .astype(low_type)
        )
    own_hidden = own_input + scatter_tensor(
        *[times_transposed(item, output_weight) for item in attended]
    )
    factor_two = lax.rsqrt(jnp.mean(own_hidden * own_hidden, axis=-1, keepdims=True) + epsilon)
    scaled_two = own_hidden * factor_two
    own_normed_two = (scaled_two * gain_feedforward).astype(low_type)
    normed_two = [jnp.concatenate(gather_tensor(own_normed_two))]
    far_normed_two = flip(own_normed_two, "dp", 1 << top)

    def feed(rows_normed, rows_cotangent):
        gate = matmul(rows_normed, gate_weight)
        upper = matmul(rows_normed, up_weight)
        grad = matmul(rows_cotangent, down_weight)
        activated, slope = gelu_parts(gate)
        hidden = (activated * upper).astype(low_type)
        grad_gate = (grad * upper * slope).astype(low_type)
        grad_up = (grad * activated).astype(low_type)
        return hidden, grad_gate, grad_up

    fed = [feed(normed_two[0], cotangents[0])]
    hidden, grad_gate, grad_up = fed[0]
    grad_two = times_transposed(grad_gate, gate_weight) + times_transposed(grad_up, up_weight)
    own_grad_two = scatter_tensor(grad_two[: 2 * rows], grad_two[2 * rows :])
    grad_scaled = own_grad_two * gain_feedforward
    inner = jnp.mean(grad_scaled * scaled_two, axis=-1, keepdims=True)
    own_grad_hidden = cotangent.astype(jnp.float32) + factor_two * (
        grad_scaled - scaled_two * inner
    )
    grad_attention = jnp.concatenate(gather_tensor(own_grad_hidden.astype(low_type)))
    grad_attended = matmul(grad_attention, output_weight).astype(low_type)

    normed_two.append(jnp.concatenate(gather_tensor(far_normed_two)))
    fed.append(feed(normed_two[1], cotangents[1]))
    down_rows = times_transposed(hidden, down_weight)
    block_output = (own_hidden + scatter_tensor(down_rows[: 2 * rows], down_rows[2 * rows :])).astype(
        low_type
    )

    def half(value):
        return lax.dynamic_slice_in_dim(value, half_start, half_width, 1)

    half_normed_two = [half(item) for item in normed_two]
    half_cotangents = [half(item) for item in cotangents]
    low_order = list(range(top))
    grad_down = reduce_weight(
        [(half_cotangents[i], fed[i][0]) for i in range(2)], low_order, dp
    )
    grad_gate_weight = reduce_weight(
        [(half_normed_two[i], fed[i][1]) for i in range(2)], low_order[::-1], dp
    )
    grad_up_weight = reduce_weight(
        [(half_normed_two[i], fed[i][2]) for i in range(2)], low_order, dp
    )
    attended_all = jnp.concatenate(attended)
    grad_output_weight = reduce_weight(
        [(grad_attention, attended_all)], [*low_order[::-1], top], dp
    )

    grad_query_list = []
    returns = [[0.0] * SPANS, [0.0] * SPANS]
    for u in range(2):
        grad_block = (
            grad_attended[u * 2 * rows : (u + 1) * 2 * rows]
            .reshape(2 * rows, heads, HEAD)
            .transpose(1, 0, 2)
        )
        window_keys, window_values = windows[u]
        scores = (
            jnp.einsum(
                "hqd,kd->hqk", query_blocks[u], window_keys, preferred_element_type=jnp.float32
            )
            * scale
        )
        scores = jnp.where(allowed[u][None], scores, negative)
        soft = jnp.exp(scores - logs[u])
        grad_soft = jnp.einsum(
            "hqd,kd->hqk", grad_block, window_values, preferred_element_type=jnp.float32
        )
        grad_scores = (
            soft * (grad_soft - jnp.sum(grad_soft * soft, axis=-1, keepdims=True))
        ).astype(low_type)
        grad_query_list.append(
            (
                jnp.einsum(
                    "hqk,kd->hqd", grad_scores, window_keys, preferred_element_type=jnp.float32
                )
                * scale
            ).transpose(1, 0, 2)
        )
        grad_keys = (
            jnp.einsum(
                "hqk,hqd->kd", grad_scores, query_blocks[u], preferred_element_type=jnp.float32
            )
            * scale
        )
        grad_values = jnp.einsum(
            "hqk,hqd->kd", soft.astype(low_type), grad_block, preferred_element_type=jnp.float32
        )
        grad_window = jnp.concatenate([grad_keys, grad_values], axis=1).reshape(
            SPANS, BLOCK, 2 * HEAD
        )
        for k in range(SPANS):
            for v in range(2):
                returns[v][k] += jnp.where(sources[u][k] == (v == 1), grad_window[k], 0.0)
    grad_query_low = (
        rotate(jnp.concatenate(grad_query_list), cosine_all[:, None, :], -sine_all[:, None, :])
        .reshape(4 * rows, heads * HEAD)
        .astype(low_type)
    )
    grad_one_part = times_transposed(grad_query_low, query_weight)
    returned = [
        jnp.stack(item).reshape(SPANS, 2, rows, 2 * HEAD).transpose(1, 0, 2, 3) for item in returns
    ]
    own_returns = scatter_tensor(*returned)[0]
    own_grad_keyval = own_returns[0]
    for k in range(1, SPANS):
        own_grad_keyval = own_grad_keyval + shift(own_returns[k].astype(low_type), -k)
    own_grad_keyval = jnp.concatenate(
        [rotate(own_grad_keyval[:, :HEAD], own_cosine, -own_sine), own_grad_keyval[:, HEAD:]],
        axis=1,
    ).astype(low_type)

    grad_query_weight = reduce_weight(
        [(normed, grad_query_low)], [*low_order, top], dp
    )
    own_grad_one = scatter_tensor(
        grad_one_part[: 2 * rows], grad_one_part[2 * rows :]
    ) + times_transposed(own_grad_keyval, keyval_weight)
    grad_scaled = own_grad_one * gain_attention
    inner = jnp.mean(grad_scaled * scaled_one, axis=-1, keepdims=True)
    grad_rows = own_grad_hidden + factor_one * (grad_scaled - scaled_one * inner)

    quarter = 2 * HEAD // 4
    grad_keyval = jnp.concatenate(gather_tensor(own_grad_keyval))
    part = lax.dynamic_slice_in_dim(grad_keyval, rank * quarter, quarter, 1)
    part = reduce_weight([(normed, part)], [*low_order, top], dp)
    pieces = jnp.stack(gather_tensor(part.T))
    order = [
        pick(pieces, 0, rank ^ g).reshape(quarter, -1) for g in range(4)
    ]
    grad_keyval_weight = jnp.concatenate(order).T

    size = width // count

    def own_block(value):
        return lax.dynamic_slice_in_dim(value, dp * size, size, 0)

    def sum_tensor(value):
        value = value + flip(value, "tensor", 1)
        return value + flip(value, "tensor", 2)

    gain_two = (
        sum_tensor(
            jnp.sum(own_block(gate_weight).astype(jnp.float32) * grad_gate_weight, axis=1)
            + jnp.sum(own_block(up_weight).astype(jnp.float32) * grad_up_weight, axis=1)
        )
        / own_block(gain_feedforward)
    )
    gain_one = (
        sum_tensor(jnp.sum(own_block(query_weight).astype(jnp.float32) * grad_query_weight, axis=1))
        + jnp.sum(own_block(keyval_weight).astype(jnp.float32) * grad_keyval_weight, axis=1)
    ) / own_block(gain_attention)
    return (
        block_output,
        grad_rows,
        gain_one,
        grad_query_weight,
        grad_keyval_weight,
        grad_output_weight,
        gain_two,
        grad_gate_weight,
        grad_up_weight,
        grad_down,
    )


def solution(mesh):
    placed = (
        P(("dp", "tensor"), None),
        P(("dp", "tensor"), None),
        P(),
        P(),
        P(None, "tensor"),
        P(),
        P(None, "tensor"),
        P(),
        P(None, "tensor"),
        P(None, "tensor"),
        P(None, "tensor"),
    )
    return jax.shard_map(
        per_device,
        mesh=mesh,
        in_specs=placed,
        out_specs=(
            P(("dp", "tensor"), None),
            P(("dp", "tensor"), None),
            P("dp"),
            P("dp", "tensor"),
            P("dp", None),
            P("dp", "tensor"),
            P("dp"),
            P("dp", "tensor"),
            P("dp", "tensor"),
            P("dp", "tensor"),
        ),
        check_vma=False,
    )
```

time: 1570 us -> 530 us (0.34)
  waiting for transfers between devices: 1230 us -> 138 us
  local copies, waits for them, and re-layouts: 45 us -> 122 us
  blocking collectives: 62 us -> 0 us
  starting transfers between devices: 1.91 us -> 47.4 us
    reduce_scatter x9 -> x0, waiting for transfers between devices: 900 us -> none  [the longest x1 211 us: per_device(): lax.psum_scatter(grad_gate_weight, 'dp', scatter_dimension=0, tiled=True)]
    psum x3 -> x0, waiting for transfers between devices: 244 us -> none  [the longest x1 84.8 us: per_device(): grad_norm_two = lax.psum(grad_norm_two_part, 'tensor')]
    ppermute x0 -> x71, waiting for transfers between devices: none -> 138 us  [the longest x63 125 us: flip(): return lax.ppermute(value, axis, [(i, i ^ bit) for i in range(count)])]
    all_gather x4 -> x0, waiting for transfers between devices: 83.9 us -> none  [the longest x1 36.4 us: per_device(): lax.all_gather(keys_own, 'dp', axis=0, tiled=True)]
    ppermute x0 -> x71, starting transfers between devices: none -> 47.4 us  [the longest x63 33.9 us: flip(): return lax.ppermute(value, axis, [(i, i ^ bit) for i in range(count)])]
    unnamed x1 -> x0, blocking collectives: 38.8 us -> none
    dynamic_slice x0 -> x23, local copies, waits for them, and re-layouts: none -> 32.2 us  [the longest x16 23.4 us: pick(): return lax.dynamic_index_in_dim(value, index, axis, keepdims=False)]
    unnamed x127 -> x294, local copies, waits for them, and re-layouts: 23.7 us -> 49.8 us
  transfers between devices with their start and end apart: 16 -> 71, of which waited for: 16 -> 20; matrix products, arithmetic and copies ran while one was open for 10% -> 61% of each run, Pallas kernels for 0% -> 0%
where the time goes in v1:
time: 530 us; the launch traced here: 521 us
  matrix products  152 us (29%)
  waiting for transfers between devices  138 us (26%)
  local copies, waits for them, and re-layouts  122 us (23%)
  other arithmetic  56.9 us (11%)
  starting transfers between devices  47.4 us (9%)
    ppermute x63, waiting for transfers between devices, flip(): return lax.ppermute(value, axis, [(i, i ^ bit) for i in range(count)])  125 us
    dot_general x30, matrix products, outer_sum(): lax.dot_general(left, right, (((0,), (0,)), ((), ())), preferred_element_...  59.9 us
    unnamed x294, local copies, waits for them, and re-layouts  49.8 us
    dot_general x9, matrix products, matmul(): return jnp.dot(left, right, preferred_element_type=jnp.float32)  42 us
    ppermute x63, starting transfers between devices, flip(): return lax.ppermute(value, axis, [(i, i ^ bit) for i in range(count)])  33.9 us
    dot_general x7, matrix products, times_transposed(): lax.dot_general(left, right, (((1,), (1,)), ((), ())), preferred_element_...  26.7 us
    dynamic_slice x16, local copies, waits for them, and re-layouts, pick(): return lax.dynamic_index_in_dim(value, index, axis, keepdims=False)  23.4 us
    ppermute x8, starting transfers between devices, shift(): lax.ppermute(value, 'dp', [(i, (i + step) % count) for i in range(count)])  13.5 us
  transfers between devices with their start and end apart: 71, of which 20 were waited for; matrix products, arithmetic and copies ran while one was open for 61% of the time, Pallas kernels for 0%

profile of v1, /device:TPU:0, one launch (start us, length us, event | category | flops | bytes accessed | tf_op | source)
XLA Modules:
  0.0 520.8 jit_solution(14044173521075370301)
XLA Ops:
  30.2 12.2 %collective-permute-done.6 = bf16[128,256]{1,0:T(8,128)(2,1)S(1)} collective-permute-done((bf16[128,256]{1,0:T(8,128)(2,1)}, bf16[128,256]{1,0:T(8,128)(2,1)S(1)}, u32[]{:S(2)}, u32[]{:S(2)}) %collective-permute-start.6) | collective-permute-done | bytes 65568 | tf_op jit(solution)/shard_map/ppermute | solution.py:39
  49.2 4.0 collective-permute-done.7
  58.8 5.6 %collective-permute-done.20 = bf16[128,2048]{0,1:T(8,128)(2,1)} collective-permute-done((bf16[128,2048]{0,1:T(8,128)(2,1)}, bf16[128,2048]{0,1:T(8,128)(2,1)}, u32[]{:S(2)}, u32[]{:S(2)}) %collective-permute-start.20) | collective-permute-done | bytes 524320 | tf_op jit(solution)/shard_map/ppermute | solution.py:34
  91.5 4.5 reshape.633
  104.9 3.5 constant_dynamic-slice_fusion.23
  108.4 10.6 %collective-permute-done.12 = bf16[128,2048]{1,0:T(8,128)(2,1)S(1)} collective-permute-done((bf16[128,2048]{1,0:T(8,128)(2,1)S(1)}, bf16[128,2048]{1,0:T(8,128)(2,1)S(1)}, u32[]{:S(2)}, u32[]{:S(2)}) %collective-permute-start.12) | collective-permute-done | bytes 524320 | tf_op jit(solution)/shard_map/ppermute | solution.py:34
  122.5 5.8 %copy.194 = bf16[512,2,2,1,256]{0,4,2,1,3:T(8,128)(2,1)} copy(bf16[512,2,2,1,256]{4,3,2,1,0:T(2,128)(2,1)} %constant_dynamic-slice_fusion.23) | data formatting | bytes 2097152
  128.3 3.6 copy.195
  136.5 8.7 %fusion.184 = f32[512,1536]{1,0:T(8,128)} fusion(bf16[512,2048]{0,1:T(8,128)(2,1)} %constant_dynamic-update-slice_fusion.29, bf16[2048,1536]{1,0:T(8,128)(2,1)} %param.21), kind=kOutput, calls=%fused_computation.426 | convolution fusion | flops 3221225472 | bytes 11534336 | tf_op jit(solution)/shard_map/dot_general | solution.py:17
  147.1 15.7 %collective-permute-done.55 = bf16[128,2048]{1,0:T(8,128)(2,1)} collective-permute-done((bf16[128,2048]{1,0:T(8,128)(2,1)}, bf16[128,2048]{1,0:T(8,128)(2,1)}, u32[]{:S(2)}, u32[]{:S(2)}) %collective-permute-start.55) | collective-permute-done | bytes 524320 | tf_op jit(solution)/shard_map/ppermute | solution.py:34
  166.6 4.8 fusion.164
  171.5 4.6 fusion.163
  176.1 9.2 %multiply_convert_fusion.5 = (bf16[512,1536]{1,0:T(8,128)(2,1)}, bf16[512,1536]{1,0:T(8,128)(2,1)S(1)}, bf16[512,1536]{1,0:T(8,128)(2,1)}) fusion(f32[512,1536]{1,0:T(8,128)S(1)} %fusion.164, f32[512,1536]{1,0:T(8,128)S(1)} %fusion.163, bf16[2048,1536]{1,0:T(8,128)(2,1)S(1)} %bitcast.508, bf16[128,2048]{0,1:T(8,128)(2,1)} %collective-permute-done.21, ...), kind=kOutput, calls=%fused_computation.25 | convolution fusion | flops 3248488448 | bytes 19398656 | tf_op jit(solution)/shard_map/dot_general | solution.py:17
  185.3 5.0 fusion.183
  203.2 5.7 %fusion.177 = (bf16[512,2048]{1,0:T(8,128)(2,1)S(1)}, f32[512,2048]{1,0:T(8,128)S(1)}) fusion(bf16[512,1536]{1,0:T(8,128)(2,1)S(1)} %copy-done.7, bf16[2048,1536]{1,0:T(8,128)(2,1)} %param.21), kind=kOutput, calls=%fused_computation.418 | convolution fusion | flops 3222274048 | bytes 14155776 | tf_op jit(solution)/shard_map/dot_general | solution.py:21
  211.1 7.1 %fusion.176 = (bf16[512,2048]{1,0:T(8,128)(2,1)S(1)}, f32[512,2048]{1,0:T(8,128)S(1)}) fusion(f32[512,2048]{1,0:T(8,128)} %fusion.183, bf16[512,1536]{1,0:T(8,128)(2,1)S(1)} %copy-done.8, bf16[2048,1536]{1,0:T(8,128)(2,1)} %param.20), kind=kOutput, calls=%fused_computation.417 | convolution fusion | flops 3223322624 | bytes 18350080 | tf_op jit(solution)/shard_map/dot_general | solution.py:21
  242.4 7.2 %multiply_convert_fusion.2 = (bf16[512,1536]{1,0:T(8,128)(2,1)}, bf16[512,1536]{1,0:T(8,128)(2,1)}, bf16[512,1536]{1,0:T(8,128)(2,1)}) fusion(f32[512,1536]{1,0:T(8,128)S(1)} %fusion.185, f32[512,1536]{1,0:T(8,128)S(1)} %copy-done.113, bf16[512,2048]{1,0:T(8,128)(2,1)S(1)} %constant_dynamic-update-slice_fusion.25, bf16[2048,1536]{1,0:T(8,128)(2,1)S(1)} %bitcast.500), kind=kOutput, calls=%fused_computation.19 | convolution fusion | flops 3240099840 | bytes 19398656 | tf_op jit(solution)/shard_map/dot_general | solution.py:17
  254.9 6.6 %collective-permute-done.18 = bf16[128,2048]{1,0:T(8,128)(2,1)} collective-permute-done((bf16[128,2048]{1,0:T(8,128)(2,1)}, bf16[128,2048]{1,0:T(8,128)(2,1)}, u32[]{:S(2)}, u32[]{:S(2)}) %collective-permute-start.18) | collective-permute-done | bytes 524320 | tf_op jit(solution)/shard_map/ppermute | solution.py:34
  261.5 4.1 fusion.168
  268.2 10.6 %collective-permute-done.26 = bf16[128,2048]{1,0:T(8,128)(2,1)S(1)} collective-permute-done((bf16[128,2048]{1,0:T(8,128)(2,1)S(1)}, bf16[128,2048]{1,0:T(8,128)(2,1)S(1)}, u32[]{:S(2)}, u32[]{:S(2)}) %collective-permute-start.26) | collective-permute-done | bytes 524320 | tf_op jit(solution)/shard_map/ppermute | solution.py:34
  289.3 3.9 multiply_reduce_fusion.1
  298.4 3.9 multiply_reduce_fusion
  309.6 5.2 fusion.178
  315.9 3.6 fusion.17
  351.0 4.5 reshape.640
  373.9 3.5 copy.203
  387.2 5.4 %collective-permute-done.33 = bf16[1,5,128,256]{3,2,1,0:T(8,128)(2,1)S(1)} collective-permute-done((bf16[1,5,128,256]{3,2,1,0:T(8,128)(2,1)S(1)}, bf16[1,5,128,256]{3,2,1,0:T(8,128)(2,1)S(1)}, u32[]{:S(2)}, u32[]{:S(2)}) %collective-permute-start.33) | collective-permute-done | bytes 327712 | tf_op jit(solution)/shard_map/ppermute | solution.py:34
  410.0 14.6 %collective-permute-done.66 = bf16[256,1536]{1,0:T(8,128)(2,1)S(1)} collective-permute-done((bf16[256,1536]{1,0:T(8,128)(2,1)S(1)}, bf16[256,1536]{1,0:T(8,128)(2,1)S(1)}, u32[]{:S(2)}, u32[]{:S(2)}) %collective-permute-start.66) | collective-permute-done | bytes 786464 | tf_op jit(solution)/shard_map/ppermute | solution.py:34
  428.8 11.3 %collective-permute-done.70 = bf16[256,1536]{1,0:T(8,128)(2,1)S(1)} collective-permute-done((bf16[256,1536]{1,0:T(8,128)(2,1)S(1)}, bf16[256,1536]{1,0:T(8,128)(2,1)S(1)}, u32[]{:S(2)}, u32[]{:S(2)}) %collective-permute-start.70) | collective-permute-done | bytes 786464 | tf_op jit(solution)/shard_map/ppermute | solution.py:34
  446.4 11.6 %collective-permute-done.68 = f32[256]{0:T(256)S(1)} collective-permute-done((f32[256]{0:T(256)S(1)}, f32[256]{0:T(256)S(1)}, u32[]{:S(2)}, u32[]{:S(2)}) %collective-permute-start.68) | collective-permute-done | bytes 1056 | tf_op jit(solution)/shard_map/ppermute | solution.py:34
  493.5 6.7 %collective-permute-done.53 = bf16[512,512]{1,0:T(8,128)(2,1)S(1)} collective-permute-done((bf16[512,512]{1,0:T(8,128)(2,1)S(1)}, bf16[512,512]{1,0:T(8,128)(2,1)S(1)}, u32[]{:S(2)}, u32[]{:S(2)}) %collective-permute-start.53) | collective-permute-done | bytes 524320 | tf_op jit(solution)/shard_map/ppermute | solution.py:34
  507.4 10.2 %collective-permute-done.54 = bf16[256,512]{1,0:T(8,128)(2,1)} collective-permute-done((bf16[256,512]{1,0:T(8,128)(2,1)}, bf16[256,512]{1,0:T(8,128)(2,1)}, u32[]{:S(2)}, u32[]{:S(2)}) %collective-permute-start.54) | collective-permute-done | bytes 262176 | tf_op jit(solution)/shard_map/ppermute | solution.py:34
  (601 shorter events, 293.1 us)
Async XLA Ops:
  3.4 53.3 %collective-permute-start.1 = (bf16[128,2048]{1,0:T(8,128)(2,1)S(1)}, bf16[128,2048]{1,0:T(8,128)(2,1)}, u32[]{:S(2)}, u32[]{:S(2)}) collective-permute-start(bf16[128,2048]{1,0:T(8,128)(2,1)S(1)} %fusion.44), channel_id=1, source_target_pairs={{0,2},{1,3},{2,0},{3,1},{4,6},{5,7},{6,4},{7,5},{8,10},{9,11},{10,... | collective-permute-start | bytes 1572872 | tf_op jit(solution)/shard_map/ppermute | solution.py:34
  6.4 52.3 %collective-permute-start = (bf16[128,2048]{1,0:T(8,128)(2,1)S(1)}, bf16[128,2048]{1,0:T(8,128)(2,1)}, u32[]{:S(2)}, u32[]{:S(2)}) collective-permute-start(bf16[128,2048]{1,0:T(8,128)(2,1)S(1)} %fusion.44), channel_id=1, source_target_pairs={{0,1},{1,0},{2,3},{3,2},{4,5},{5,4},{6,7},{7,6},{8,9},{9,8},{10,11... | collective-permute-start | bytes 1572872 | tf_op jit(solution)/shard_map/ppermute | solution.py:34
  24.7 17.8 %collective-permute-start.6 = (bf16[128,256]{1,0:T(8,128)(2,1)}, bf16[128,256]{1,0:T(8,128)(2,1)S(1)}, u32[]{:S(2)}, u32[]{:S(2)}) collective-permute-start(bf16[128,256]{1,0:T(8,128)(2,1)} %pad_maximum_fusion.12), channel_id=1, source_target_pairs={{0,16},{4,20},{8,24},{12,28},{16,0},{20,4},{24,8},{28,12},{1,17},{... | collective-permute-start | bytes 196616 | tf_op jit(solution)/shard_map/ppermute | solution.py:39
  26.8 27.4 %collective-permute-start.59 = (bf16[128,2048]{0,1:T(8,128)(2,1)}, bf16[128,2048]{0,1:T(8,128)(2,1)}, u32[]{:S(2)}, u32[]{:S(2)}) collective-permute-start(bf16[128,2048]{0,1:T(8,128)(2,1)} %copy.135), channel_id=1, source_target_pairs={{0,16},{4,20},{8,24},{12,28},{16,0},{20,4},{24,8},{28,12},{1,17},{... | collective-permute-start | bytes 1572872 | tf_op jit(solution)/shard_map/ppermute | solution.py:34
  54.2 34.0 %collective-permute-start.19 = (bf16[128,2048]{0,1:T(8,128)(2,1)}, bf16[128,2048]{0,1:T(8,128)(2,1)}, u32[]{:S(2)}, u32[]{:S(2)}) collective-permute-start(bf16[128,2048]{0,1:T(8,128)(2,1)} %copy.135), channel_id=1, source_target_pairs={{0,1},{1,0},{2,3},{3,2},{4,5},{5,4},{6,7},{7,6},{8,9},{9,8},{10,11... | collective-permute-start | bytes 1572872 | tf_op jit(solution)/shard_map/ppermute | solution.py:34
  56.7 45.0 %collective-permute-start.60 = (bf16[128,2048]{0,1:T(8,128)(2,1)}, bf16[128,2048]{0,1:T(8,128)(2,1)}, u32[]{:S(2)}, u32[]{:S(2)}) collective-permute-start(bf16[128,2048]{0,1:T(8,128)(2,1)} %collective-permute-done.59), channel_id=1, source_target_pairs={{0,1},{1,0},{2,3},{3,2},{4,5},{5,4},{6,7},{7,6},{8,9},{9,8},{10,11... | collective-permute-start | bytes 1572872 | tf_op jit(solution)/shard_map/ppermute | solution.py:34
  58.6 42.8 %collective-permute-start.61 = (bf16[128,2048]{0,1:T(8,128)(2,1)}, bf16[128,2048]{0,1:T(8,128)(2,1)}, u32[]{:S(2)}, u32[]{:S(2)}) collective-permute-start(bf16[128,2048]{0,1:T(8,128)(2,1)} %collective-permute-done.59), channel_id=1, source_target_pairs={{0,2},{1,3},{2,0},{3,1},{4,6},{5,7},{6,4},{7,5},{8,10},{9,11},{10,... | collective-permute-start | bytes 1572872 | tf_op jit(solution)/shard_map/ppermute | solution.py:34
  64.4 24.2 %collective-permute-start.21 = (bf16[128,2048]{0,1:T(8,128)(2,1)}, bf16[128,2048]{0,1:T(8,128)(2,1)}, u32[]{:S(2)}, u32[]{:S(2)}) collective-permute-start(bf16[128,2048]{0,1:T(8,128)(2,1)} %collective-permute-done.20), channel_id=1, source_target_pairs={{0,1},{1,0},{2,3},{3,2},{4,5},{5,4},{6,7},{7,6},{8,9},{9,8},{10,11... | collective-permute-start | bytes 1572872 | tf_op jit(solution)/shard_map/ppermute | solution.py:34
  80.2 23.4 %collective-permute-start.11 = (bf16[128,2048]{1,0:T(8,128)(2,1)S(1)}, bf16[128,2048]{1,0:T(8,128)(2,1)}, u32[]{:S(2)}, u32[]{:S(2)}) collective-permute-start(bf16[128,2048]{1,0:T(8,128)(2,1)S(1)} %slice.652), channel_id=1, source_target_pairs={{0,1},{1,0},{2,3},{3,2},{4,5},{5,4},{6,7},{7,6},{8,9},{9,8},{10,11... | collective-permute-start | bytes 1572872 | tf_op jit(solution)/shard_map/ppermute | solution.py:34
  88.2 20.2 %collective-permute-start.10 = (bf16[128,2048]{1,0:T(8,128)(2,1)S(1)}, bf16[128,2048]{1,0:T(8,128)(2,1)}, u32[]{:S(2)}, u32[]{:S(2)}) collective-permute-start(bf16[128,2048]{1,0:T(8,128)(2,1)S(1)} %slice.653), channel_id=1, source_target_pairs={{0,1},{1,0},{2,3},{3,2},{4,5},{5,4},{6,7},{7,6},{8,9},{9,8},{10,11... | collective-permute-start | bytes 1572872 | tf_op jit(solution)/shard_map/ppermute | solution.py:34
  101.5 32.5 %collective-permute-start.62 = (bf16[128,2048]{0,1:T(8,128)(2,1)}, bf16[128,2048]{0,1:T(8,128)(2,1)}, u32[]{:S(2)}, u32[]{:S(2)}) collective-permute-start(bf16[128,2048]{0,1:T(8,128)(2,1)} %collective-permute-done.61), channel_id=1, source_target_pairs={{0,1},{1,0},{2,3},{3,2},{4,5},{5,4},{6,7},{7,6},{8,9},{9,8},{10,11... | collective-permute-start | bytes 1572872 | tf_op jit(solution)/shard_map/ppermute | solution.py:34
  136.0 30.6 %collective-permute-start.13 = (bf16[128,2048]{1,0:T(8,128)(2,1)}, bf16[128,2048]{1,0:T(8,128)(2,1)S(1)}, u32[]{:S(2)}, u32[]{:S(2)}) collective-permute-start(bf16[128,2048]{1,0:T(8,128)(2,1)} %multiply_convert_fusion.8), channel_id=1, source_target_pairs={{0,1},{1,0},{2,3},{3,2},{4,5},{5,4},{6,7},{7,6},{8,9},{9,8},{10,11... | collective-permute-start | bytes 1572872 | tf_op jit(solution)/shard_map/ppermute | solution.py:34
  136.0 26.8 %collective-permute-start.55 = (bf16[128,2048]{1,0:T(8,128)(2,1)}, bf16[128,2048]{1,0:T(8,128)(2,1)}, u32[]{:S(2)}, u32[]{:S(2)}) collective-permute-start(bf16[128,2048]{1,0:T(8,128)(2,1)} %multiply_convert_fusion.8), channel_id=1, source_target_pairs={{0,16},{4,20},{8,24},{12,28},{16,0},{20,4},{24,8},{28,12},{1,17},{... | collective-permute-start | bytes 1572872 | tf_op jit(solution)/shard_map/ppermute | solution.py:34
  136.1 30.5 %collective-permute-start.15 = (bf16[128,2048]{1,0:T(8,128)(2,1)}, bf16[128,2048]{1,0:T(8,128)(2,1)S(1)}, u32[]{:S(2)}, u32[]{:S(2)}) collective-permute-start(bf16[128,2048]{1,0:T(8,128)(2,1)} %collective-permute-done.14), channel_id=1, source_target_pairs={{0,1},{1,0},{2,3},{3,2},{4,5},{5,4},{6,7},{7,6},{8,9},{9,8},{10,11... | collective-permute-start | bytes 1572872 | tf_op jit(solution)/shard_map/ppermute | solution.py:34
  162.8 67.7 %collective-permute-start.56 = (bf16[128,2048]{1,0:T(8,128)(2,1)}, bf16[128,2048]{1,0:T(8,128)(2,1)}, u32[]{:S(2)}, u32[]{:S(2)}) collective-permute-start(bf16[128,2048]{1,0:T(8,128)(2,1)} %collective-permute-done.55), channel_id=1, source_target_pairs={{0,1},{1,0},{2,3},{3,2},{4,5},{5,4},{6,7},{7,6},{8,9},{9,8},{10,11... | collective-permute-start | bytes 1572872 | tf_op jit(solution)/shard_map/ppermute | solution.py:34
  162.8 67.9 %collective-permute-start.57 = (bf16[128,2048]{1,0:T(8,128)(2,1)}, bf16[128,2048]{1,0:T(8,128)(2,1)}, u32[]{:S(2)}, u32[]{:S(2)}) collective-permute-start(bf16[128,2048]{1,0:T(8,128)(2,1)} %collective-permute-done.55), channel_id=1, source_target_pairs={{0,2},{1,3},{2,0},{3,1},{4,6},{5,7},{6,4},{7,5},{8,10},{9,11},{10,... | collective-permute-start | bytes 1572872 | tf_op jit(solution)/shard_map/ppermute | solution.py:34
  219.2 33.6 %collective-permute-start.22 = (bf16[128,2048]{1,0:T(8,128)(2,1)}, bf16[128,2048]{1,0:T(8,128)(2,1)}, u32[]{:S(2)}, u32[]{:S(2)}) collective-permute-start(bf16[128,2048]{1,0:T(8,128)(2,1)} %get-tuple-element.78), channel_id=1, source_target_pairs={{0,1},{1,0},{2,3},{3,2},{4,5},{5,4},{6,7},{7,6},{8,9},{9,8},{10,11... | collective-permute-start | bytes 1572872 | tf_op jit(solution)/shard_map/ppermute | solution.py:34
  230.5 24.4 %collective-permute-start.16 = (bf16[128,2048]{1,0:T(8,128)(2,1)}, bf16[128,2048]{1,0:T(8,128)(2,1)}, u32[]{:S(2)}, u32[]{:S(2)}) collective-permute-start(bf16[128,2048]{1,0:T(8,128)(2,1)} %get-tuple-element.80), channel_id=1, source_target_pairs={{0,1},{1,0},{2,3},{3,2},{4,5},{5,4},{6,7},{7,6},{8,9},{9,8},{10,11... | collective-permute-start | bytes 1572872 | tf_op jit(solution)/shard_map/ppermute | solution.py:34
  237.1 24.4 %collective-permute-start.18 = (bf16[128,2048]{1,0:T(8,128)(2,1)}, bf16[128,2048]{1,0:T(8,128)(2,1)}, u32[]{:S(2)}, u32[]{:S(2)}) collective-permute-start(bf16[128,2048]{1,0:T(8,128)(2,1)} %fusion.57), channel_id=1, source_target_pairs={{0,2},{1,3},{2,0},{3,1},{4,6},{5,7},{6,4},{7,5},{8,10},{9,11},{10,... | collective-permute-start | bytes 1572872 | tf_op jit(solution)/shard_map/ppermute | solution.py:34
  268.1 109.3 %collective-permute-start.63 = (bf16[512,1536]{1,0:T(8,128)(2,1)}, bf16[512,1536]{1,0:T(8,128)(2,1)}, u32[]{:S(2)}, u32[]{:S(2)}) collective-permute-start(bf16[512,1536]{1,0:T(8,128)(2,1)} %fusion.6), channel_id=1, source_target_pairs={{0,8},{4,12},{8,0},{12,4},{16,24},{20,28},{24,16},{28,20},{1,9},{5... | collective-permute-start | bytes 4718600 | tf_op jit(solution)/shard_map/ppermute | solution.py:34
  281.1 101.6 %collective-permute-start.65 = (bf16[512,1536]{1,0:T(8,128)(2,1)}, bf16[512,1536]{1,0:T(8,128)(2,1)}, u32[]{:S(2)}, u32[]{:S(2)}) collective-permute-start(bf16[512,1536]{1,0:T(8,128)(2,1)} %fusion.7), channel_id=1, source_target_pairs={{0,4},{4,0},{8,12},{12,8},{16,20},{20,16},{24,28},{28,24},{1,5},{5... | collective-permute-start | bytes 4718600 | tf_op jit(solution)/shard_map/ppermute | solution.py:34
  284.2 100.8 %collective-permute-start.69 = (bf16[512,1536]{1,0:T(8,128)(2,1)}, bf16[512,1536]{1,0:T(8,128)(2,1)}, u32[]{:S(2)}, u32[]{:S(2)}) collective-permute-start(bf16[512,1536]{1,0:T(8,128)(2,1)} %fusion.8), channel_id=1, source_target_pairs={{0,4},{4,0},{8,12},{12,8},{16,20},{20,16},{24,28},{28,24},{1,5},{5... | collective-permute-start | bytes 4718600 | tf_op jit(solution)/shard_map/ppermute | solution.py:34
  315.8 83.3 %collective-permute-start.29 = (bf16[128,2048]{1,0:T(8,128)(2,1)}, bf16[128,2048]{1,0:T(8,128)(2,1)}, u32[]{:S(2)}, u32[]{:S(2)}) collective-permute-start(bf16[128,2048]{1,0:T(8,128)(2,1)} %get-tuple-element.77), channel_id=1, source_target_pairs={{0,1},{1,0},{2,3},{3,2},{4,5},{5,4},{6,7},{7,6},{8,9},{9,8},{10,11... | collective-permute-start | bytes 1572872 | tf_op jit(solution)/shard_map/ppermute | solution.py:34
  344.3 36.0 %collective-permute-start.32 = (bf16[1,5,128,256]{3,2,1,0:T(8,128)(2,1)}, bf16[1,5,128,256]{3,2,1,0:T(8,128)(2,1)}, u32[]{:S(2)}, u32[]{:S(2)}) collective-permute-start(bf16[1,5,128,256]{3,2,1,0:T(8,128)(2,1)} %slice.654), channel_id=1, source_target_pairs={{0,1},{1,0},{2,3},{3,2},{4,5},{5,4},{6,7},{7,6},{8,9},{9,8},{10,11... | collective-permute-start | bytes 983048 | tf_op jit(solution)/shard_map/ppermute | solution.py:34
  380.4 26.0 %collective-permute-start.64 = (bf16[256,1536]{1,0:T(8,128)(2,1)S(1)}, bf16[256,1536]{1,0:T(8,128)(2,1)S(1)}, u32[]{:S(2)}, u32[]{:S(2)}) collective-permute-start(bf16[256,1536]{1,0:T(8,128)(2,1)S(1)} %fusion.29), channel_id=1, source_target_pairs={{0,4},{4,0},{8,12},{12,8},{16,20},{20,16},{24,28},{28,24},{1,5},{5... | collective-permute-start | bytes 2359304 | tf_op jit(solution)/shard_map/ppermute | solution.py:34
  402.7 65.6 %collective-permute-start.28 = (bf16[128,2048]{1,0:T(8,128)(2,1)}, bf16[128,2048]{1,0:T(8,128)(2,1)}, u32[]{:S(2)}, u32[]{:S(2)}) collective-permute-start(bf16[128,2048]{1,0:T(8,128)(2,1)} %get-tuple-element.76), channel_id=1, source_target_pairs={{0,1},{1,0},{2,3},{3,2},{4,5},{5,4},{6,7},{7,6},{8,9},{9,8},{10,11... | collective-permute-start | bytes 1572872 | tf_op jit(solution)/shard_map/ppermute | solution.py:34
  402.7 69.3 %collective-permute-start.38 = (bf16[1024,512]{1,0:T(8,128)(2,1)}, bf16[1024,512]{1,0:T(8,128)(2,1)}, u32[]{:S(2)}, u32[]{:S(2)}) collective-permute-start(bf16[1024,512]{1,0:T(8,128)(2,1)} %convolution_convert_fusion.1), channel_id=1, source_target_pairs={{0,4},{4,0},{8,12},{12,8},{16,20},{20,16},{24,28},{28,24},{1,5},{5... | collective-permute-start | bytes 3145736 | tf_op jit(solution)/shard_map/ppermute | solution.py:34
  404.1 20.4 %collective-permute-start.66 = (bf16[256,1536]{1,0:T(8,128)(2,1)S(1)}, bf16[256,1536]{1,0:T(8,128)(2,1)S(1)}, u32[]{:S(2)}, u32[]{:S(2)}) collective-permute-start(bf16[256,1536]{1,0:T(8,128)(2,1)S(1)} %fusion.27), channel_id=1, source_target_pairs={{0,8},{4,12},{8,0},{12,4},{16,24},{20,28},{24,16},{28,20},{1,9},{5... | collective-permute-start | bytes 2359304 | tf_op jit(solution)/shard_map/ppermute | solution.py:34
  404.4 35.8 %collective-permute-start.70 = (bf16[256,1536]{1,0:T(8,128)(2,1)S(1)}, bf16[256,1536]{1,0:T(8,128)(2,1)S(1)}, u32[]{:S(2)}, u32[]{:S(2)}) collective-permute-start(bf16[256,1536]{1,0:T(8,128)(2,1)S(1)} %fusion.25), channel_id=1, source_target_pairs={{0,8},{4,12},{8,0},{12,4},{16,24},{20,28},{24,16},{28,20},{1,9},{5... | collective-permute-start | bytes 2359304 | tf_op jit(solution)/shard_map/ppermute | solution.py:34
  406.4 37.2 %collective-permute-start.43 = (bf16[128,256]{1,0:T(8,128)(2,1)S(1)}, bf16[128,256]{1,0:T(8,128)(2,1)S(1)}, u32[]{:S(2)}, u32[]{:S(2)}) collective-permute-start(bf16[128,256]{1,0:T(8,128)(2,1)S(1)} %pad_maximum_fusion.13), channel_id=1, source_target_pairs={{0,1},{1,0},{2,3},{3,2},{4,5},{5,4},{6,7},{7,6},{8,9},{9,8},{10,11... | collective-permute-start | bytes 196616 | tf_op jit(solution)/shard_map/ppermute | solution.py:34
  443.1 38.4 %collective-permute-start.52 = (bf16[1024,512]{1,0:T(8,128)(2,1)}, bf16[1024,512]{1,0:T(8,128)(2,1)}, u32[]{:S(2)}, u32[]{:S(2)}) collective-permute-start(bf16[1024,512]{1,0:T(8,128)(2,1)} %convolution_convert_fusion), channel_id=1, source_target_pairs={{0,8},{4,12},{8,0},{12,4},{16,24},{20,28},{24,16},{28,20},{1,9},{5... | collective-permute-start | bytes 3145736 | tf_op jit(solution)/shard_map/ppermute | solution.py:34
  443.6 24.7 %collective-permute-start.30 = (bf16[128,2048]{1,0:T(8,128)(2,1)}, bf16[128,2048]{1,0:T(8,128)(2,1)}, u32[]{:S(2)}, u32[]{:S(2)}) collective-permute-start(bf16[128,2048]{1,0:T(8,128)(2,1)} %fusion.50), channel_id=1, source_target_pairs={{0,2},{1,3},{2,0},{3,1},{4,6},{5,7},{6,4},{7,5},{8,10},{9,11},{10,... | collective-permute-start | bytes 1572872 | tf_op jit(solution)/shard_map/ppermute | solution.py:34
  (169 other events, 1507.0 us)
